TPU v7x, 32 devices: a whole 2x2x4 slice. The times are simulated.
32 devices in a mesh: irrep: 4 (over z), row: 8 (over y, x, core).
Axes of the slice: x: 2, y: 2, z: 4, core: 2. Of those that a mesh axis runs over, the one named last changes fastest.
Arguments:
- densities: float32 [4, 2048, 512], P('irrep', 'row'), may hold values from -6 to 6
- reduced_kernel: float32 [4, 12288, 2048], P('irrep', 'row'), may hold values from -0.125 to 0.125
Outputs:
- potentials: float32 [4, 12288, 512], P('irrep', 'row')
All inputs are finite; a program needn't handle non-finite values.
Results may differ from a plain program's by a relative error of at most 0.000086.
Values sent between devices are 32-bit elements; how exact they have to be, the bound alone decides.
No kernel may reach another device: no remote copies, remote signals or barrier semaphores. Data moves between devices by JAX's collectives and lax.ppermute only.
A program may use at most 128 MiB of HBM per device.

v0:
```python
import math

import jax
import jax.numpy as jnp
from jax import lax
from jax.sharding import PartitionSpec as P


def partner_2(value, axis, stride):
    mask = 2**stride
    pairs = [(source, source ^ mask) for source in range(lax.axis_size(axis))]
    return lax.ppermute(value, axis, pairs)


def body(densities, reduced_kernel):
    octants = lax.axis_size("irrep")
    norm_scale = 1.0 / math.sqrt(octants)
    kernel_tile = reduced_kernel[0]
    holding = densities[0]
    octant_index = lax.axis_index("irrep")
    for level in range(octants.bit_length() - 1):
        partner = partner_2(holding, "irrep", level)
        upper_half = octant_index >> level & 1
        holding = jnp.where(upper_half == 1, partner - holding, holding + partner)
    folded = holding * norm_scale
    summed = jnp.dot(
        kernel_tile,
        lax.all_gather(folded, "row", axis=0, tiled=True),
        precision=lax.Precision.HIGHEST,
        preferred_element_type=jnp.float32,
    )
    return summed[None]


def solution(mesh):
    placed = (P("irrep", "row", None), P("irrep", "row", None))
    return jax.shard_map(
        body, mesh=mesh, in_specs=placed, out_specs=P("irrep", "row", None), check_vma=False
    )
```

profile of v0, /device:TPU:0, one launch (start us, length us, event | category | flops | bytes accessed | tf_op | source)
XLA Modules:
  0.0 138.3 jit_solution(14005285927682056465)
XLA Ops:
  6.5 0.0 all-gather.2.cloned.1.call-start
  6.5 3.0 %collective-permute-start = (f32[256,512]{1,0:T(8,128)}, f32[256,512]{1,0:T(8,128)S(1)}, u32[]{:S(2)}, u32[]{:S(2)}) collective-permute-start(f32[256,512]{1,0:T(8,128)} %bitcast.12), channel_id=1, source_target_pairs={{0,8},{8,0},{16,24},{24,16},{1,9},{9,1},{17,25},{25,17},{2,10},{10... | collective-permute-start | bytes 1572872 | tf_op jit(solution)/shard_map/ppermute | solution.py:12
  9.6 12.1 %collective-permute-done = f32[256,512]{1,0:T(8,128)S(1)} collective-permute-done((f32[256,512]{1,0:T(8,128)}, f32[256,512]{1,0:T(8,128)S(1)}, u32[]{:S(2)}, u32[]{:S(2)}) %collective-permute-start) | collective-permute-done | bytes 524320 | tf_op jit(solution)/shard_map/ppermute | solution.py:12
  21.7 1.1 add_select_fusion
  22.8 2.8 %collective-permute-start.1 = (f32[256,512]{1,0:T(8,128)S(1)}, f32[256,512]{1,0:T(8,128)S(1)}, u32[]{:S(2)}, u32[]{:S(2)}) collective-permute-start(f32[256,512]{1,0:T(8,128)S(1)} %add_select_fusion), channel_id=1, source_target_pairs={{0,16},{8,24},{16,0},{24,8},{1,17},{9,25},{17,1},{25,9},{2,18},{10... | collective-permute-start | bytes 1572872 | tf_op jit(solution)/shard_map/ppermute | solution.py:12
  25.7 22.5 %collective-permute-done.1 = f32[256,512]{1,0:T(8,128)S(1)} collective-permute-done((f32[256,512]{1,0:T(8,128)S(1)}, f32[256,512]{1,0:T(8,128)S(1)}, u32[]{:S(2)}, u32[]{:S(2)}) %collective-permute-start.1) | collective-permute-done | bytes 524320 | tf_op jit(solution)/shard_map/ppermute | solution.py:12
  48.1 0.9 select_multiply_fusion
  49.0 0.0 all-gather.2.cloned.1.call-update
  49.1 37.9 %all-gather.2.cloned.1.call-done = f32[2048,512]{1,0:T(8,128)} async-done(((f32[256,512]{1,0:T(8,128)}), f32[2048,512]{1,0:T(8,128)}) %all-gather.2.cloned.1.call-update) | async-done | bytes 4194320 | tf_op jit(solution)/shard_map/all_gather | solution.py:28
  86.9 42.2 %fusion.2 = f32[1,1536,512]{1,2,0:T(8,128)S(1)} fusion(f32[2048,512]{1,0:T(8,128)} %all-gather.2.cloned.1.call-done, f32[1,1536,2048]{2,1,0:T(8,128)} %param.3), kind=kOutput, calls=%fused_computation.2 | convolution fusion | flops 19327352832 | bytes 19922944 | tf_op jit(solution)/shard_map/dot_general | solution.py:26
  129.1 2.4 %copy.3 = f32[1,1536,512]{2,1,0:T(8,128)} copy(f32[1,1536,512]{1,2,0:T(8,128)S(1)} %fusion.2) | data formatting | bytes 6291456 | tf_op jit(solution)/shard_map/broadcast_in_dim | solution.py:32
Async XLA Ops:
  6.5 80.4 %all-gather.2.cloned.1.call-start = ((), (), s32[]{:S(2)}) async-start(), calls=%async_computation | async-start | bytes 4718592 | tf_op jit(solution)/shard_map/all_gather | solution.py:28
  6.5 15.2 %collective-permute-start = (f32[256,512]{1,0:T(8,128)}, f32[256,512]{1,0:T(8,128)S(1)}, u32[]{:S(2)}, u32[]{:S(2)}) collective-permute-start(f32[256,512]{1,0:T(8,128)} %bitcast.12), channel_id=1, source_target_pairs={{0,8},{8,0},{16,24},{24,16},{1,9},{9,1},{17,25},{25,17},{2,10},{10... | collective-permute-start | bytes 1572872 | tf_op jit(solution)/shard_map/ppermute | solution.py:12
  22.8 25.3 %collective-permute-start.1 = (f32[256,512]{1,0:T(8,128)S(1)}, f32[256,512]{1,0:T(8,128)S(1)}, u32[]{:S(2)}, u32[]{:S(2)}) collective-permute-start(f32[256,512]{1,0:T(8,128)S(1)} %add_select_fusion), channel_id=1, source_target_pairs={{0,16},{8,24},{16,0},{24,8},{1,17},{9,25},{17,1},{25,9},{2,18},{10... | collective-permute-start | bytes 1572872 | tf_op jit(solution)/shard_map/ppermute | solution.py:12
Sparse Core Ops, SparseCore 0:
  49.2 37.6 all-gather.1
where the time goes:
time: 138 us
  waiting for transfers between devices  72.5 us (53%)
  matrix products  42.2 us (31%)
  between operations  13.4 us (10%)
  starting transfers between devices  5.85 us (4%)
  local copies, waits for them, and re-layouts  2.37 us (2%)
  other arithmetic  2.03 us (1%)
    dot_general x1, matrix products, body(): jnp.dot(kernel_tile, lax.all_gather(folded, 'row', axis=0, tiled=True), p...  42.2 us
    all_gather x1, waiting for transfers between devices, body(): lax.all_gather(folded, 'row', axis=0, tiled=True)  37.9 us
    ppermute x2, waiting for transfers between devices, partner_2(): return lax.ppermute(value, axis, pairs)  34.6 us
    ppermute x2, starting transfers between devices, partner_2(): return lax.ppermute(value, axis, pairs)  5.84 us
  transfers between devices with their start and end apart: 3, of which 3 were waited for; matrix products, arithmetic and copies ran while one was open for 0% of the time, Pallas kernels for 0%

commit v1 on v0

v1 whole, which is shorter than its diff:
```python
import functools
import math

import jax
import jax.numpy as jnp
from jax import lax
from jax.experimental import pallas as pl
from jax.experimental.pallas import tpu as pltpu
from jax.sharding import PartitionSpec as P

HIGH = jnp.bfloat16


def exchange(value, axis, bit):
    mask = 1 << bit
    pairs = [(source, source ^ mask) for source in range(lax.axis_size(axis))]
    return lax.ppermute(value, axis, pairs)


def in_two(value):
    high = value.astype(HIGH)
    return high, (value - high.astype(jnp.float32)).astype(HIGH)


def split_kernel(halves, owners, k_ref, high_ref, low_ref):
    width = k_ref.shape[1] // owners // halves
    for owner in range(owners):
        for half in range(halves):
            start = (owner * halves + half) * width
            high, low = in_two(k_ref[:, start : start + width])
            at = (owner // 2) * width
            high_ref[half, owner % 2, :, at : at + width] = high
            low_ref[half, owner % 2, :, at : at + width] = low


def split(k, halves, owners):
    rows, sources = k.shape
    tile = 128
    shape = (halves, 2, rows, sources // halves // 2)
    block = pl.BlockSpec((halves, 2, tile, shape[3]), lambda m: (0, 0, m, 0))
    return pl.pallas_call(
        functools.partial(split_kernel, halves, owners),
        grid=(rows // tile,),
        in_specs=[pl.BlockSpec((tile, sources), lambda m: (m, 0))],
        out_specs=[block, block],
        out_shape=[jax.ShapeDtypeStruct(shape, HIGH)] * 2,
        cost_estimate=pl.CostEstimate(
            flops=4 * rows * sources, bytes_accessed=8 * rows * sources, transcendentals=0
        ),
        compiler_params=pltpu.CompilerParams(vmem_limit_bytes=48 * 2**20),
        name="split_reduced_kernel",
    )(k)


def multiply_kernel(units, depth, pieces, accumulate, me_ref, *refs):
    refs = list(refs)
    highs, lows = refs[:units], refs[units : 2 * units]
    del refs[: 2 * units]
    flat = [[refs.pop(0) for _ in of] for of in pieces]
    before = refs.pop(0) if accumulate else None
    out_ref, f_high, f_low = refs
    me = me_ref[0]

    @pl.when(pl.program_id(0) == 0)
    def _():
        for unit, of in enumerate(pieces):
            for ref, (rels, offset) in zip(flat[unit], of):
                for at, rel in enumerate(rels):
                    high, low = in_two(ref[at])
                    start = ((me ^ rel) >> 1) * depth + offset
                    rows = pl.ds(pl.multiple_of(start, 16), ref.shape[1])
                    f_high[unit, rows, :] = high
                    f_low[unit, rows, :] = low

    total = before[0] if accumulate else None
    for unit in range(units):
        high, low = highs[unit][0, 0], lows[unit][0, 0]
        dot = functools.partial(jnp.dot, preferred_element_type=jnp.float32)
        part = dot(high, f_low[unit]) + dot(low, f_high[unit]) + dot(high, f_high[unit])
        total = part if total is None else total + part
    out_ref[0] = total


def multiply(me, k_high, k_low, units, column, columns, before, accumulate):
    rows, deep = k_high.shape[2:]
    width = units[0][2][0][0].shape[2]
    tile = 256
    depth = 2 * deep // lax.axis_size("row")

    def block(half, core):
        return pl.BlockSpec(
            (1, 1, tile, deep), lambda m, me: (half, (me[0] & 1) ^ core, m, 0)
        )

    blocks = [block(half, core) for half, core, _ in units]
    arrays = [array for _, _, of in units for array, _, _ in of]
    pieces = [[(tuple(rels), offset) for _, rels, offset in of] for _, _, of in units]
    whole = [pl.BlockSpec(a.shape, lambda m, me, n=a.ndim: (0,) * n) for a in arrays]
    place = pl.BlockSpec((1, tile, width), lambda m, me: (0, m, column))
    extra, extra_specs, alias = [], [], {}
    if before is not None:
        extra = [before]
        extra_specs = [place if accumulate else pl.BlockSpec(memory_space=pl.ANY)]
        alias = {1 + 2 * len(units) + len(arrays): 0}

    def kernel(me_ref, *refs):
        refs = list(refs)
        if before is not None and not accumulate:
            del refs[2 * len(units) + len(arrays)]
        multiply_kernel(len(units), depth, pieces, accumulate, me_ref, *refs)

    return pl.pallas_call(
        kernel,
        grid_spec=pltpu.PrefetchScalarGridSpec(
            num_scalar_prefetch=1,
            grid=(rows // tile,),
            in_specs=blocks + blocks + whole + extra_specs,
            out_specs=place,
            scratch_shapes=[pltpu.VMEM((len(units), deep, width), HIGH)] * 2,
        ),
        out_shape=jax.ShapeDtypeStruct((1, rows, columns), jnp.float32),
        input_output_aliases=alias,
        cost_estimate=pl.CostEstimate(
            flops=6 * rows * deep * width * len(units),
            bytes_accessed=4 * rows * deep * len(units) + 4 * rows * width,
            transcendentals=0,
        ),
        compiler_params=pltpu.CompilerParams(vmem_limit_bytes=48 * 2**20),
        name="multiply_sources",
    )(me, *[k_high] * len(units), *[k_low] * len(units), *arrays, *extra)


def fold(holding, levels, order):
    octants = lax.axis_size("irrep")
    octant = lax.axis_index("irrep")
    for step in range(levels):
        bit = (step + order) % levels
        partner = exchange(holding, "irrep", bit)
        upper = octant >> bit & 1
        holding = jnp.where(upper == 1, partner - holding, holding + partner)
    return holding * (1.0 / math.sqrt(octants))


def gather_chips(piece, bits, order):
    rels, held = [0], piece[None]
    for step in range(bits):
        bit = 1 + (step + order) % bits
        held = jnp.concatenate([held, exchange(held, "row", bit)])
        rels = rels + [rel ^ (1 << bit) for rel in rels]
    return held, rels


def body(densities, reduced_kernel):
    owners = lax.axis_size("row")
    levels = lax.axis_size("irrep").bit_length() - 1
    bits = owners.bit_length() - 2
    mine = densities[0]
    deep, columns = mine.shape
    halves, parts = 2, 2
    rows, width = deep // halves, columns // parts
    me = lax.axis_index("row").astype(jnp.int32).reshape(1)

    k_high, k_low = split(reduced_kernel[0], halves, owners)
    out = None
    for part in range(parts):
        units = []
        for half in range(halves):
            chunk = mine[half * rows : (half + 1) * rows, part * width : (part + 1) * width]
            number = part * halves + half
            folded = fold(chunk, levels, 1 if number == 1 else 0)
            if number == parts * halves - 1:
                pieces = [
                    (*gather_chips(folded[: rows // 2], bits, 0), 0),
                    (*gather_chips(folded[rows // 2 :], bits, 1), rows // 2),
                ]
            else:
                pieces = [(*gather_chips(folded, bits, number % 2), 0)]
            other = [
                (exchange(array, "row", 0), [rel ^ 1 for rel in rels], offset)
                for array, rels, offset in pieces
            ]
            units.append((half, 0, pieces))
            units.append((half, 1, other))
        if part < parts - 1:
            out = multiply(me, k_high, k_low, units, part, columns, out, False)
        else:
            out = multiply(me, k_high, k_low, units[:2], part, columns, out, False)
            out = multiply(me, k_high, k_low, units[2:3], part, columns, out, True)
            out = multiply(me, k_high, k_low, units[3:], part, columns, out, True)
    return out


def solution(mesh):
    placed = (P("irrep", "row", None), P("irrep", "row", None))
    return jax.shard_map(
        body, mesh=mesh, in_specs=placed, out_specs=P("irrep", "row", None), check_vma=False
    )
```

time: 138 us -> 101 us (0.73); the launches traced: 138 us -> 99.8 us
  waiting for transfers between devices: 72.5 us -> 24.5 us
  Pallas kernels: 0 us -> 43.2 us
  matrix products: 42.2 us -> 0 us
  starting transfers between devices: 5.85 us -> 29.2 us
  between operations: 13.4 us -> 0.16 us
    pallas_call x0 -> x5, Pallas kernels: none -> 43.2 us  [the longest x4 29.4 us: multiply(): pl.pallas_call(kernel, grid_spec=pltpu.PrefetchScalarGridSpec(num_scalar_...]
    dot_general x1 -> x0, matrix products: 42.2 us -> none  [body(): jnp.dot(kernel_tile, lax.all_gather(folded, 'row', axis=0, tiled=True), p...]
    all_gather x1 -> x0, waiting for transfers between devices: 37.9 us -> none  [body(): lax.all_gather(folded, 'row', axis=0, tiled=True)]
    ppermute x2 -> x23, starting transfers between devices: 5.84 us -> 29.2 us  [exchange(): return lax.ppermute(value, axis, pairs)]
    ppermute x2 -> x23, waiting for transfers between devices: 34.6 us -> 24.5 us  [exchange(): return lax.ppermute(value, axis, pairs)]
    broadcast_in_dim x1, local copies, waits for them, and re-layouts: 2.37 us -> 0.01 us  [gather_chips(): rels, held = ([0], piece[None])]
  transfers between devices with their start and end apart: 3 -> 23, of which waited for: 3 -> 9; matrix products, arithmetic and copies ran while one was open for 0% -> 0% of each run, Pallas kernels for 0% -> 37%
where the time goes in v1:
time: 101 us; the launch traced here: 99.8 us
  Pallas kernels  43.2 us (43%)
  starting transfers between devices  29.2 us (29%)
  waiting for transfers between devices  24.5 us (24%)
  other arithmetic  1.47 us (1%)
  local copies, waits for them, and re-layouts  1.14 us (1%)
    pallas_call x4, Pallas kernels, multiply(): pl.pallas_call(kernel, grid_spec=pltpu.PrefetchScalarGridSpec(num_scalar_...  29.4 us
    ppermute x23, starting transfers between devices, exchange(): return lax.ppermute(value, axis, pairs)  29.2 us
    ppermute x23, waiting for transfers between devices, exchange(): return lax.ppermute(value, axis, pairs)  24.5 us
    pallas_call x1, Pallas kernels, split(): pl.pallas_call(functools.partial(split_kernel, halves, owners), grid=(row...  13.8 us
  transfers between devices with their start and end apart: 23, of which 9 were waited for; matrix products, arithmetic and copies ran while one was open for 0% of the time, Pallas kernels for 37%

profile of v1, /device:TPU:0, one launch (start us, length us, event | category | flops | bytes accessed | tf_op | source)
XLA Modules:
  0.0 99.8 jit_solution(51742148779879557)
XLA Ops:
  0.0 1.1 %fusion = (f32[128,256]{1,0:T(8,128)S(1)}, f32[128,256]{1,0:T(8,128)S(1)}, f32[128,256]{1,0:T(8,128)S(1)}, f32[128,256]{1,0:T(8,128)S(1)}) fusion(f32[256,512]{1,0:T(8,128)} %bitcast.14), kind=kLoop, calls=%fused_computation.20 | loop fusion | bytes 1048576 | tf_op jit(solution)/shard_map/slice | solution.py:168
  1.1 3.1 %collective-permute-start = (f32[128,256]{1,0:T(8,128)S(1)}, f32[128,256]{1,0:T(8,128)S(1)}, u32[]{:S(2)}, u32[]{:S(2)}) collective-permute-start(f32[128,256]{1,0:T(8,128)S(1)} %get-tuple-element.16), channel_id=1, source_target_pairs={{0,8},{8,0},{16,24},{24,16},{1,9},{9,1},{17,25},{25,17},{2,10},{10... | collective-permute-start | bytes 393224 | tf_op jit(solution)/shard_map/ppermute | solution.py:17
  4.2 0.1 collective-permute-start.13
  4.3 3.0 %collective-permute-start.18 = (f32[128,256]{1,0:T(8,128)S(1)}, f32[128,256]{1,0:T(8,128)S(1)}, u32[]{:S(2)}, u32[]{:S(2)}) collective-permute-start(f32[128,256]{1,0:T(8,128)S(1)} %get-tuple-element.13), channel_id=1, source_target_pairs={{0,16},{8,24},{16,0},{24,8},{1,17},{9,25},{17,1},{25,9},{2,18},{10... | collective-permute-start | bytes 393224 | tf_op jit(solution)/shard_map/ppermute | solution.py:17
  7.3 1.6 %collective-permute-start.8 = (f32[128,256]{1,0:T(8,128)S(1)}, f32[128,256]{1,0:T(8,128)S(1)}, u32[]{:S(2)}, u32[]{:S(2)}) collective-permute-start(f32[128,256]{1,0:T(8,128)S(1)} %get-tuple-element.15), channel_id=1, source_target_pairs={{0,8},{8,0},{16,24},{24,16},{1,9},{9,1},{17,25},{25,17},{2,10},{10... | collective-permute-start | bytes 393224 | tf_op jit(solution)/shard_map/ppermute | solution.py:17
  8.8 2.5 %collective-permute-done = f32[128,256]{1,0:T(8,128)S(1)} collective-permute-done((f32[128,256]{1,0:T(8,128)S(1)}, f32[128,256]{1,0:T(8,128)S(1)}, u32[]{:S(2)}, u32[]{:S(2)}) %collective-permute-start) | collective-permute-done | bytes 131104 | tf_op jit(solution)/shard_map/ppermute | solution.py:17
  11.4 2.8 %collective-permute-done.13 = f32[128,256]{1,0:T(8,128)S(1)} collective-permute-done((f32[128,256]{1,0:T(8,128)S(1)}, f32[128,256]{1,0:T(8,128)S(1)}, u32[]{:S(2)}, u32[]{:S(2)}) %collective-permute-start.13) | collective-permute-done | bytes 131104 | tf_op jit(solution)/shard_map/ppermute | solution.py:17
  14.2 0.0 collective-permute-done.18
  14.2 2.0 %collective-permute-done.8 = f32[128,256]{1,0:T(8,128)S(1)} collective-permute-done((f32[128,256]{1,0:T(8,128)S(1)}, f32[128,256]{1,0:T(8,128)S(1)}, u32[]{:S(2)}, u32[]{:S(2)}) %collective-permute-start.8) | collective-permute-done | bytes 131104 | tf_op jit(solution)/shard_map/ppermute | solution.py:17
  16.1 1.2 %add_select_fusion = (f32[128,256]{1,0:T(8,128)S(1)}, f32[128,256]{1,0:T(8,128)S(1)}, f32[128,256]{1,0:T(8,128)S(1)}, f32[128,256]{1,0:T(8,128)S(1)}) fusion(f32[128,256]{1,0:T(8,128)S(1)} %collective-permute-done.18, pred[]{:T(512)S(6)} %eq.4, f32[256,512]{1,0:T(8,128)} %bitcast.15, f32[128,256]{1,0:T(8,128)S(1)} %collective-permute-done, pred[]{:T(512)S(6)} %eq.5, ...), kind=kLoop, calls=%fused_computation.11 | loop fusion | flops 393216 | bytes 1572866 | tf_op jit(solution)/shard_map/jit(_where)/select_n | solution.py:140
  17.3 1.8 %collective-permute-start.19 = (f32[128,256]{1,0:T(8,128)S(1)}, f32[128,256]{1,0:T(8,128)S(1)}, u32[]{:S(2)}, u32[]{:S(2)}) collective-permute-start(f32[128,256]{1,0:T(8,128)S(1)} %get-tuple-element.9), channel_id=1, source_target_pairs={{0,8},{8,0},{16,24},{24,16},{1,9},{9,1},{17,25},{25,17},{2,10},{10... | collective-permute-start | bytes 393224 | tf_op jit(solution)/shard_map/ppermute | solution.py:17
  19.1 2.6 %collective-permute-start.14 = (f32[128,256]{1,0:T(8,128)S(1)}, f32[128,256]{1,0:T(8,128)S(1)}, u32[]{:S(2)}, u32[]{:S(2)}) collective-permute-start(f32[128,256]{1,0:T(8,128)S(1)} %get-tuple-element.12), channel_id=1, source_target_pairs={{0,16},{8,24},{16,0},{24,8},{1,17},{9,25},{17,1},{25,9},{2,18},{10... | collective-permute-start | bytes 393224 | tf_op jit(solution)/shard_map/ppermute | solution.py:17
  21.7 0.3 collective-permute-start.9
  22.0 2.6 %collective-permute-start.1 = (f32[128,256]{1,0:T(8,128)S(1)}, f32[128,256]{1,0:T(8,128)S(1)}, u32[]{:S(2)}, u32[]{:S(2)}) collective-permute-start(f32[128,256]{1,0:T(8,128)S(1)} %get-tuple-element.10), channel_id=1, source_target_pairs={{0,16},{8,24},{16,0},{24,8},{1,17},{9,25},{17,1},{25,9},{2,18},{10... | collective-permute-start | bytes 393224 | tf_op jit(solution)/shard_map/ppermute | solution.py:17
  24.6 0.0 collective-permute-done.19
  24.7 1.6 %collective-permute-start.20 = (f32[1,128,256]{2,1,0:T(8,128)S(1)}, f32[1,128,256]{2,1,0:T(8,128)S(1)}, u32[]{:S(2)}, u32[]{:S(2)}) collective-permute-start(f32[1,128,256]{2,1,0:T(8,128)S(1)} %multiply_bitcast_fusion), channel_id=1, source_target_pairs={{0,4},{1,5},{2,6},{3,7},{4,0},{5,1},{6,2},{7,3},{8,12},{9,13},{10,... | collective-permute-start | bytes 393224 | tf_op jit(solution)/shard_map/ppermute | solution.py:17
  26.2 7.8 %collective-permute-done.14 = f32[128,256]{1,0:T(8,128)S(1)} collective-permute-done((f32[128,256]{1,0:T(8,128)S(1)}, f32[128,256]{1,0:T(8,128)S(1)}, u32[]{:S(2)}, u32[]{:S(2)}) %collective-permute-start.14) | collective-permute-done | bytes 131104 | tf_op jit(solution)/shard_map/ppermute | solution.py:17
  34.0 1.6 %collective-permute-start.15 = (f32[1,128,256]{2,1,0:T(8,128)S(1)}, f32[1,128,256]{2,1,0:T(8,128)S(1)}, u32[]{:S(2)}, u32[]{:S(2)}) collective-permute-start(f32[1,128,256]{2,1,0:T(8,128)S(1)} %multiply_bitcast_fusion.1), channel_id=1, source_target_pairs={{0,2},{1,3},{2,0},{3,1},{4,6},{5,7},{6,4},{7,5},{8,10},{9,11},{10,... | collective-permute-start | bytes 393224 | tf_op jit(solution)/shard_map/ppermute | solution.py:17
  35.6 1.2 %collective-permute-done.9 = f32[128,256]{1,0:T(8,128)S(1)} collective-permute-done((f32[128,256]{1,0:T(8,128)S(1)}, f32[128,256]{1,0:T(8,128)S(1)}, u32[]{:S(2)}, u32[]{:S(2)}) %collective-permute-start.9) | collective-permute-done | bytes 131104 | tf_op jit(solution)/shard_map/ppermute | solution.py:17
  36.8 1.6 %collective-permute-start.10 = (f32[1,128,256]{2,1,0:T(8,128)S(1)}, f32[1,128,256]{2,1,0:T(8,128)S(1)}, u32[]{:S(2)}, u32[]{:S(2)}) collective-permute-start(f32[1,128,256]{2,1,0:T(8,128)S(1)} %multiply_bitcast_fusion.2), channel_id=1, source_target_pairs={{0,2},{1,3},{2,0},{3,1},{4,6},{5,7},{6,4},{7,5},{8,10},{9,11},{10,... | collective-permute-start | bytes 393224 | tf_op jit(solution)/shard_map/ppermute | solution.py:17
  38.4 0.0 collective-permute-done.1
  38.4 0.0 collective-permute-done.20
  38.4 1.4 %collective-permute-start.21 = (f32[2,128,256]{2,1,0:T(8,128)S(1)}, f32[2,128,256]{2,1,0:T(8,128)S(1)}, u32[]{:S(2)}, u32[]{:S(2)}) collective-permute-start(f32[2,128,256]{2,1,0:T(8,128)S(1)} %pad_maximum_fusion.7), channel_id=1, source_target_pairs={{0,2},{1,3},{2,0},{3,1},{4,6},{5,7},{6,4},{7,5},{8,10},{9,11},{10,... | collective-permute-start | bytes 786440 | tf_op jit(solution)/shard_map/ppermute | solution.py:17
  39.8 0.0 collective-permute-done.15
  39.8 1.6 %collective-permute-start.16 = (f32[2,128,256]{2,1,0:T(8,128)S(1)}, f32[2,128,256]{2,1,0:T(8,128)S(1)}, u32[]{:S(2)}, u32[]{:S(2)}) collective-permute-start(f32[2,128,256]{2,1,0:T(8,128)S(1)} %pad_maximum_fusion.6), channel_id=1, source_target_pairs={{0,4},{1,5},{2,6},{3,7},{4,0},{5,1},{6,2},{7,3},{8,12},{9,13},{10,... | collective-permute-start | bytes 786440 | tf_op jit(solution)/shard_map/ppermute | solution.py:17
  41.4 0.6 collective-permute-start.5
  42.0 1.2 %collective-permute-start.2 = (f32[1,64,256]{2,1,0:T(8,128)S(1)}, f32[1,64,256]{2,1,0:T(8,128)S(1)}, u32[]{:S(2)}, u32[]{:S(2)}) collective-permute-start(f32[1,64,256]{2,1,0:T(8,128)S(1)} %get-tuple-element.18), channel_id=1, source_target_pairs={{0,2},{1,3},{2,0},{3,1},{4,6},{5,7},{6,4},{7,5},{8,10},{9,11},{10,... | collective-permute-start | bytes 196616 | tf_op jit(solution)/shard_map/ppermute | solution.py:17
  43.2 0.0 collective-permute-done.10
  43.3 1.6 %collective-permute-start.11 = (f32[2,128,256]{2,1,0:T(8,128)S(1)}, f32[2,128,256]{2,1,0:T(8,128)S(1)}, u32[]{:S(2)}, u32[]{:S(2)}) collective-permute-start(f32[2,128,256]{2,1,0:T(8,128)S(1)} %pad_maximum_fusion.5), channel_id=1, source_target_pairs={{0,4},{1,5},{2,6},{3,7},{4,0},{5,1},{6,2},{7,3},{8,12},{9,13},{10,... | collective-permute-start | bytes 786440 | tf_op jit(solution)/shard_map/ppermute | solution.py:17
  44.8 2.5 %collective-permute-done.21 = f32[2,128,256]{2,1,0:T(8,128)S(1)} collective-permute-done((f32[2,128,256]{2,1,0:T(8,128)S(1)}, f32[2,128,256]{2,1,0:T(8,128)S(1)}, u32[]{:S(2)}, u32[]{:S(2)}) %collective-permute-start.21) | collective-permute-done | bytes 262176 | tf_op jit(solution)/shard_map/ppermute | solution.py:17
  47.3 0.1 collective-permute-start.22
  47.4 1.7 %collective-permute-done.16 = f32[2,128,256]{2,1,0:T(8,128)S(1)} collective-permute-done((f32[2,128,256]{2,1,0:T(8,128)S(1)}, f32[2,128,256]{2,1,0:T(8,128)S(1)}, u32[]{:S(2)}, u32[]{:S(2)}) %collective-permute-start.16) | collective-permute-done | bytes 262176 | tf_op jit(solution)/shard_map/ppermute | solution.py:17
  49.2 0.1 collective-permute-start.17
  49.3 1.3 %collective-permute-done.5 = f32[1,64,256]{2,1,0:T(8,128)S(1)} collective-permute-done((f32[1,64,256]{2,1,0:T(8,128)S(1)}, f32[1,64,256]{2,1,0:T(8,128)S(1)}, u32[]{:S(2)}, u32[]{:S(2)}) %collective-permute-start.5) | collective-permute-done | bytes 65568 | tf_op jit(solution)/shard_map/ppermute | solution.py:17
  50.6 0.8 collective-permute-start.6
  51.3 13.8 %split_reduced_kernel.1 = (bf16[2,2,1536,512]{3,2,1,0:T(8,128)(2,1)}, bf16[2,2,1536,512]{3,2,1,0:T(8,128)(2,1)}) custom-call(f32[1536,2048]{1,0:T(8,128)} %bitcast.13), custom_call_target="tpu_custom_call" | custom-call | flops 12582912 | bytes 25165824 | tf_op jit(solution)/shard_map/split_reduced_kernel/pallas_call | solution.py:41
  65.2 0.0 collective-permute-done.2
  65.2 1.6 %collective-permute-start.3 = (f32[2,64,256]{2,1,0:T(8,128)S(1)}, f32[2,64,256]{2,1,0:T(8,128)S(1)}, u32[]{:S(2)}, u32[]{:S(2)}) collective-permute-start(f32[2,64,256]{2,1,0:T(8,128)S(1)} %pad_maximum_fusion.8), channel_id=1, source_target_pairs={{0,4},{1,5},{2,6},{3,7},{4,0},{5,1},{6,2},{7,3},{8,12},{9,13},{10,... | collective-permute-start | bytes 393224 | tf_op jit(solution)/shard_map/ppermute | solution.py:17
  66.8 0.0 collective-permute-done.6
  66.8 0.1 collective-permute-start.7
  66.9 0.0 collective-permute-done.11
  66.9 0.5 collective-permute-start.12
  67.5 2.7 %collective-permute-done.3 = f32[2,64,256]{2,1,0:T(8,128)S(1)} collective-permute-done((f32[2,64,256]{2,1,0:T(8,128)S(1)}, f32[2,64,256]{2,1,0:T(8,128)S(1)}, u32[]{:S(2)}, u32[]{:S(2)}) %collective-permute-start.3) | collective-permute-done | bytes 131104 | tf_op jit(solution)/shard_map/ppermute | solution.py:17
  70.2 0.1 collective-permute-start.4
  70.3 0.0 collective-permute-done.22.refs_11_
  70.3 0.0 collective-permute-done.17.refs_9_
  70.3 10.0 %multiply_sources.4.refs_6_ = f32[1,1536,512]{2,1,0:T(8,128)} custom-call(s32[1]{0:T(128)} %bitcast.me_ref, bf16[2,2,1536,512]{3,2,1,0:T(8,128)(2,1)} %get-tuple-element.7.refs_0_.refs_1_.refs_2_.refs_3_, bf16[2,2,1536,512]{3,2,1,0:T(8,128)(2,1)} %get-tuple-element.7.refs_0_.refs_1_.refs_2_.refs_3_, ...), custom_call_target="tpu_custom_call" | custom-call | flops 4831838208 | bytes 14155776 | tf_op jit(solution)/shard_map/multiply_sources/pallas_call | solution.py:112
  80.3 0.0 collective-permute-done.12.refs_5_
  80.3 7.1 %multiply_sources.5.refs_4_ = f32[1,1536,512]{2,1,0:T(8,128)} custom-call(s32[1]{0:T(128)} %bitcast.me_ref, bf16[2,2,1536,512]{3,2,1,0:T(8,128)(2,1)} %get-tuple-element.7.refs_0_.refs_1_.refs_2_.refs_3_, bf16[2,2,1536,512]{3,2,1,0:T(8,128)(2,1)} %get-tuple-element.7.refs_0_.refs_1_.refs_2_.refs_3_, ...), custom_call_target="tpu_custom_call", output_to_operand_aliasing={{}: (7, {})} | custom-call | flops 2415919104 | bytes 7864320 | tf_op jit(solution)/shard_map/multiply_sources/pallas_call | solution.py:112
  87.4 6.1 %multiply_sources.6.refs_4_ = f32[1,1536,512]{2,1,0:T(8,128)} custom-call(s32[1]{0:T(128)} %bitcast.me_ref, bf16[2,2,1536,512]{3,2,1,0:T(8,128)(2,1)} %get-tuple-element.7.refs_0_.refs_1_.refs_2_.refs_3_, bf16[2,2,1536,512]{3,2,1,0:T(8,128)(2,1)} %get-tuple-element.8.refs_4_.refs_5_.refs_6_.refs_7_.refs_2_.refs_3_.refs_1_, ...), custom_call_target="tpu_custom_call", output_to_operand_aliasing={{}: (5, {})} | custom-call | flops 1207959552 | bytes 4718592 | tf_op jit(solution)/shard_map/multiply_sources/pallas_call | solution.py:112
  93.6 0.0 collective-permute-done.7.refs_3_
  93.6 0.0 collective-permute-done.4.refs_2_
  93.6 6.2 %multiply_sources.7 = f32[1,1536,512]{2,1,0:T(8,128)} custom-call(s32[1]{0:T(128)} %bitcast.me_ref, bf16[2,2,1536,512]{3,2,1,0:T(8,128)(2,1)} %get-tuple-element.7.refs_0_.refs_1_.refs_2_.refs_3_, bf16[2,2,1536,512]{3,2,1,0:T(8,128)(2,1)} %get-tuple-element.8.refs_4_.refs_5_.refs_6_.refs_7_.refs_2_.refs_3_.refs_1_, ...), custom_call_target="tpu_custom_call", output_to_operand_aliasing={{}: (5, {})} | custom-call | flops 1207959552 | bytes 4718592 | tf_op jit(solution)/shard_map/multiply_sources/pallas_call | solution.py:112
  (15 shorter events, 0.3 us)
Async XLA Ops:
  1.1 10.2 %collective-permute-start = (f32[128,256]{1,0:T(8,128)S(1)}, f32[128,256]{1,0:T(8,128)S(1)}, u32[]{:S(2)}, u32[]{:S(2)}) collective-permute-start(f32[128,256]{1,0:T(8,128)S(1)} %get-tuple-element.16), channel_id=1, source_target_pairs={{0,8},{8,0},{16,24},{24,16},{1,9},{9,1},{17,25},{25,17},{2,10},{10... | collective-permute-start | bytes 393224 | tf_op jit(solution)/shard_map/ppermute | solution.py:17
  4.2 9.9 %collective-permute-start.13 = (f32[128,256]{1,0:T(8,128)S(1)}, f32[128,256]{1,0:T(8,128)S(1)}, u32[]{:S(2)}, u32[]{:S(2)}) collective-permute-start(f32[128,256]{1,0:T(8,128)S(1)} %get-tuple-element.14), channel_id=1, source_target_pairs={{0,8},{8,0},{16,24},{24,16},{1,9},{9,1},{17,25},{25,17},{2,10},{10... | collective-permute-start | bytes 393224 | tf_op jit(solution)/shard_map/ppermute | solution.py:17
  4.3 9.9 %collective-permute-start.18 = (f32[128,256]{1,0:T(8,128)S(1)}, f32[128,256]{1,0:T(8,128)S(1)}, u32[]{:S(2)}, u32[]{:S(2)}) collective-permute-start(f32[128,256]{1,0:T(8,128)S(1)} %get-tuple-element.13), channel_id=1, source_target_pairs={{0,16},{8,24},{16,0},{24,8},{1,17},{9,25},{17,1},{25,9},{2,18},{10... | collective-permute-start | bytes 393224 | tf_op jit(solution)/shard_map/ppermute | solution.py:17
  7.3 8.9 %collective-permute-start.8 = (f32[128,256]{1,0:T(8,128)S(1)}, f32[128,256]{1,0:T(8,128)S(1)}, u32[]{:S(2)}, u32[]{:S(2)}) collective-permute-start(f32[128,256]{1,0:T(8,128)S(1)} %get-tuple-element.15), channel_id=1, source_target_pairs={{0,8},{8,0},{16,24},{24,16},{1,9},{9,1},{17,25},{25,17},{2,10},{10... | collective-permute-start | bytes 393224 | tf_op jit(solution)/shard_map/ppermute | solution.py:17
  17.3 7.3 %collective-permute-start.19 = (f32[128,256]{1,0:T(8,128)S(1)}, f32[128,256]{1,0:T(8,128)S(1)}, u32[]{:S(2)}, u32[]{:S(2)}) collective-permute-start(f32[128,256]{1,0:T(8,128)S(1)} %get-tuple-element.9), channel_id=1, source_target_pairs={{0,8},{8,0},{16,24},{24,16},{1,9},{9,1},{17,25},{25,17},{2,10},{10... | collective-permute-start | bytes 393224 | tf_op jit(solution)/shard_map/ppermute | solution.py:17
  19.1 14.9 %collective-permute-start.14 = (f32[128,256]{1,0:T(8,128)S(1)}, f32[128,256]{1,0:T(8,128)S(1)}, u32[]{:S(2)}, u32[]{:S(2)}) collective-permute-start(f32[128,256]{1,0:T(8,128)S(1)} %get-tuple-element.12), channel_id=1, source_target_pairs={{0,16},{8,24},{16,0},{24,8},{1,17},{9,25},{17,1},{25,9},{2,18},{10... | collective-permute-start | bytes 393224 | tf_op jit(solution)/shard_map/ppermute | solution.py:17
  21.7 15.1 %collective-permute-start.9 = (f32[128,256]{1,0:T(8,128)S(1)}, f32[128,256]{1,0:T(8,128)S(1)}, u32[]{:S(2)}, u32[]{:S(2)}) collective-permute-start(f32[128,256]{1,0:T(8,128)S(1)} %get-tuple-element.11), channel_id=1, source_target_pairs={{0,16},{8,24},{16,0},{24,8},{1,17},{9,25},{17,1},{25,9},{2,18},{10... | collective-permute-start | bytes 393224 | tf_op jit(solution)/shard_map/ppermute | solution.py:17
  22.0 16.3 %collective-permute-start.1 = (f32[128,256]{1,0:T(8,128)S(1)}, f32[128,256]{1,0:T(8,128)S(1)}, u32[]{:S(2)}, u32[]{:S(2)}) collective-permute-start(f32[128,256]{1,0:T(8,128)S(1)} %get-tuple-element.10), channel_id=1, source_target_pairs={{0,16},{8,24},{16,0},{24,8},{1,17},{9,25},{17,1},{25,9},{2,18},{10... | collective-permute-start | bytes 393224 | tf_op jit(solution)/shard_map/ppermute | solution.py:17
  24.7 13.7 %collective-permute-start.20 = (f32[1,128,256]{2,1,0:T(8,128)S(1)}, f32[1,128,256]{2,1,0:T(8,128)S(1)}, u32[]{:S(2)}, u32[]{:S(2)}) collective-permute-start(f32[1,128,256]{2,1,0:T(8,128)S(1)} %multiply_bitcast_fusion), channel_id=1, source_target_pairs={{0,4},{1,5},{2,6},{3,7},{4,0},{5,1},{6,2},{7,3},{8,12},{9,13},{10,... | collective-permute-start | bytes 393224 | tf_op jit(solution)/shard_map/ppermute | solution.py:17
  34.0 5.8 %collective-permute-start.15 = (f32[1,128,256]{2,1,0:T(8,128)S(1)}, f32[1,128,256]{2,1,0:T(8,128)S(1)}, u32[]{:S(2)}, u32[]{:S(2)}) collective-permute-start(f32[1,128,256]{2,1,0:T(8,128)S(1)} %multiply_bitcast_fusion.1), channel_id=1, source_target_pairs={{0,2},{1,3},{2,0},{3,1},{4,6},{5,7},{6,4},{7,5},{8,10},{9,11},{10,... | collective-permute-start | bytes 393224 | tf_op jit(solution)/shard_map/ppermute | solution.py:17
  36.8 6.4 %collective-permute-start.10 = (f32[1,128,256]{2,1,0:T(8,128)S(1)}, f32[1,128,256]{2,1,0:T(8,128)S(1)}, u32[]{:S(2)}, u32[]{:S(2)}) collective-permute-start(f32[1,128,256]{2,1,0:T(8,128)S(1)} %multiply_bitcast_fusion.2), channel_id=1, source_target_pairs={{0,2},{1,3},{2,0},{3,1},{4,6},{5,7},{6,4},{7,5},{8,10},{9,11},{10,... | collective-permute-start | bytes 393224 | tf_op jit(solution)/shard_map/ppermute | solution.py:17
  38.4 8.9 %collective-permute-start.21 = (f32[2,128,256]{2,1,0:T(8,128)S(1)}, f32[2,128,256]{2,1,0:T(8,128)S(1)}, u32[]{:S(2)}, u32[]{:S(2)}) collective-permute-start(f32[2,128,256]{2,1,0:T(8,128)S(1)} %pad_maximum_fusion.7), channel_id=1, source_target_pairs={{0,2},{1,3},{2,0},{3,1},{4,6},{5,7},{6,4},{7,5},{8,10},{9,11},{10,... | collective-permute-start | bytes 786440 | tf_op jit(solution)/shard_map/ppermute | solution.py:17
  39.8 9.3 %collective-permute-start.16 = (f32[2,128,256]{2,1,0:T(8,128)S(1)}, f32[2,128,256]{2,1,0:T(8,128)S(1)}, u32[]{:S(2)}, u32[]{:S(2)}) collective-permute-start(f32[2,128,256]{2,1,0:T(8,128)S(1)} %pad_maximum_fusion.6), channel_id=1, source_target_pairs={{0,4},{1,5},{2,6},{3,7},{4,0},{5,1},{6,2},{7,3},{8,12},{9,13},{10,... | collective-permute-start | bytes 786440 | tf_op jit(solution)/shard_map/ppermute | solution.py:17
  41.4 9.1 %collective-permute-start.5 = (f32[1,64,256]{2,1,0:T(8,128)S(1)}, f32[1,64,256]{2,1,0:T(8,128)S(1)}, u32[]{:S(2)}, u32[]{:S(2)}) collective-permute-start(f32[1,64,256]{2,1,0:T(8,128)S(1)} %get-tuple-element.17), channel_id=1, source_target_pairs={{0,4},{1,5},{2,6},{3,7},{4,0},{5,1},{6,2},{7,3},{8,12},{9,13},{10,... | collective-permute-start | bytes 196616 | tf_op jit(solution)/shard_map/ppermute | solution.py:17
  42.0 23.2 %collective-permute-start.2 = (f32[1,64,256]{2,1,0:T(8,128)S(1)}, f32[1,64,256]{2,1,0:T(8,128)S(1)}, u32[]{:S(2)}, u32[]{:S(2)}) collective-permute-start(f32[1,64,256]{2,1,0:T(8,128)S(1)} %get-tuple-element.18), channel_id=1, source_target_pairs={{0,2},{1,3},{2,0},{3,1},{4,6},{5,7},{6,4},{7,5},{8,10},{9,11},{10,... | collective-permute-start | bytes 196616 | tf_op jit(solution)/shard_map/ppermute | solution.py:17
  43.3 23.6 %collective-permute-start.11 = (f32[2,128,256]{2,1,0:T(8,128)S(1)}, f32[2,128,256]{2,1,0:T(8,128)S(1)}, u32[]{:S(2)}, u32[]{:S(2)}) collective-permute-start(f32[2,128,256]{2,1,0:T(8,128)S(1)} %pad_maximum_fusion.5), channel_id=1, source_target_pairs={{0,4},{1,5},{2,6},{3,7},{4,0},{5,1},{6,2},{7,3},{8,12},{9,13},{10,... | collective-permute-start | bytes 786440 | tf_op jit(solution)/shard_map/ppermute | solution.py:17
  47.3 23.0 %collective-permute-start.22 = (f32[4,128,256]{2,1,0:T(8,128)S(1)}, f32[4,128,256]{2,1,0:T(8,128)S(1)}, u32[]{:S(2)}, u32[]{:S(2)}) collective-permute-start(f32[4,128,256]{2,1,0:T(8,128)S(1)} %pad_maximum_fusion.2.refs_10_), channel_id=1, source_target_pairs={{0,1},{1,0},{2,3},{3,2},{4,5},{5,4},{6,7},{7,6},{8,9},{9,8},{10,11... | collective-permute-start | bytes 1572872 | tf_op jit(solution)/shard_map/ppermute | solution.py:17
  49.2 21.1 %collective-permute-start.17 = (f32[4,128,256]{2,1,0:T(8,128)S(1)}, f32[4,128,256]{2,1,0:T(8,128)S(1)}, u32[]{:S(2)}, u32[]{:S(2)}) collective-permute-start(f32[4,128,256]{2,1,0:T(8,128)S(1)} %pad_maximum_fusion.1.refs_8_), channel_id=1, source_target_pairs={{0,1},{1,0},{2,3},{3,2},{4,5},{5,4},{6,7},{7,6},{8,9},{9,8},{10,11... | collective-permute-start | bytes 1572872 | tf_op jit(solution)/shard_map/ppermute | solution.py:17
  50.6 16.2 %collective-permute-start.6 = (f32[2,64,256]{2,1,0:T(8,128)S(1)}, f32[2,64,256]{2,1,0:T(8,128)S(1)}, u32[]{:S(2)}, u32[]{:S(2)}) collective-permute-start(f32[2,64,256]{2,1,0:T(8,128)S(1)} %pad_maximum_fusion.9), channel_id=1, source_target_pairs={{0,2},{1,3},{2,0},{3,1},{4,6},{5,7},{6,4},{7,5},{8,10},{9,11},{10,... | collective-permute-start | bytes 393224 | tf_op jit(solution)/shard_map/ppermute | solution.py:17
  65.2 5.0 %collective-permute-start.3 = (f32[2,64,256]{2,1,0:T(8,128)S(1)}, f32[2,64,256]{2,1,0:T(8,128)S(1)}, u32[]{:S(2)}, u32[]{:S(2)}) collective-permute-start(f32[2,64,256]{2,1,0:T(8,128)S(1)} %pad_maximum_fusion.8), channel_id=1, source_target_pairs={{0,4},{1,5},{2,6},{3,7},{4,0},{5,1},{6,2},{7,3},{8,12},{9,13},{10,... | collective-permute-start | bytes 393224 | tf_op jit(solution)/shard_map/ppermute | solution.py:17
  66.8 26.8 %collective-permute-start.7 = (f32[4,64,256]{2,1,0:T(8,128)S(1)}, f32[4,64,256]{2,1,0:T(8,128)S(1)}, u32[]{:S(2)}, u32[]{:S(2)}) collective-permute-start(f32[4,64,256]{2,1,0:T(8,128)S(1)} %pad_maximum_fusion.4.refs_3_), channel_id=1, source_target_pairs={{0,1},{1,0},{2,3},{3,2},{4,5},{5,4},{6,7},{7,6},{8,9},{9,8},{10,11... | collective-permute-start | bytes 786440 | tf_op jit(solution)/shard_map/ppermute | solution.py:17
  66.9 13.4 %collective-permute-start.12 = (f32[4,128,256]{2,1,0:T(8,128)S(1)}, f32[4,128,256]{2,1,0:T(8,128)S(1)}, u32[]{:S(2)}, u32[]{:S(2)}) collective-permute-start(f32[4,128,256]{2,1,0:T(8,128)S(1)} %pad_maximum_fusion.refs_4_), channel_id=1, source_target_pairs={{0,1},{1,0},{2,3},{3,2},{4,5},{5,4},{6,7},{7,6},{8,9},{9,8},{10,11... | collective-permute-start | bytes 1572872 | tf_op jit(solution)/shard_map/ppermute | solution.py:17
  70.2 23.4 %collective-permute-start.4 = (f32[4,64,256]{2,1,0:T(8,128)S(1)}, f32[4,64,256]{2,1,0:T(8,128)S(1)}, u32[]{:S(2)}, u32[]{:S(2)}) collective-permute-start(f32[4,64,256]{2,1,0:T(8,128)S(1)} %pad_maximum_fusion.3.refs_2_), channel_id=1, source_target_pairs={{0,1},{1,0},{2,3},{3,2},{4,5},{5,4},{6,7},{7,6},{8,9},{9,8},{10,11... | collective-permute-start | bytes 786440 | tf_op jit(solution)/shard_map/ppermute | solution.py:17

commit v2 on v0

v2 whole, which is shorter than its diff:
```python
import functools
import math

import jax
import jax.numpy as jnp
from jax import lax
from jax.experimental import pallas as pl
from jax.experimental.pallas import tpu as pltpu
from jax.sharding import PartitionSpec as P

HALF = jnp.bfloat16
AXES = ("irrep", "row")


def exchange(value, masks):
    devices = lax.axis_size("irrep") * lax.axis_size("row")
    pairs = [(at, at ^ masks[at & 1]) for at in range(devices)]
    return lax.ppermute(value, AXES, pairs)


def turns(step, count):
    return [(step + core) % count for core in range(2)]


def fold(holding, levels):
    owners, octant = lax.axis_size("row"), lax.axis_index("irrep")
    core = lax.axis_index("row") & 1
    for step in range(levels):
        bits = turns(step, levels)
        partner = exchange(holding, [owners << bit for bit in bits])
        upper = octant >> jnp.where(core == 1, bits[1], bits[0]) & 1
        holding = jnp.where(upper == 1, partner - holding, holding + partner)
    return holding * (1.0 / math.sqrt(lax.axis_size("irrep")))


def gather_chips(piece, bits):
    held = piece[None]
    for step in range(bits):
        masks = [2 << bit for bit in turns(step, bits)]
        held = jnp.concatenate([held, exchange(held, masks)])
    return held


def owner_table(bits):
    me = lax.axis_index("row").astype(jnp.int32)
    core = me & 1
    table = []
    for other in range(2):
        for at in range(1 << bits):
            rel = [other, other]
            for step in range(bits):
                if at >> step & 1:
                    for side, bit in enumerate(turns(step, bits)):
                        rel[side] ^= 2 << bit
            table.append(me ^ jnp.where(core ^ other == 1, rel[1], rel[0]))
    return jnp.stack(table).astype(jnp.int32)


def in_two(value):
    high = value.astype(HALF)
    return high, (value - high.astype(jnp.float32)).astype(HALF)


def multiply_kernel(owners, arrays, accumulate, table_ref, *refs):
    refs = list(refs)
    k_refs = [refs.pop(0) for _ in range(owners)]
    f_refs = [refs.pop(0) for _ in range(arrays)]
    before = refs.pop(0) if accumulate else None
    out_ref, f_high, f_low = refs
    depth = k_refs[0].shape[1]

    @pl.when(pl.program_id(0) == 0)
    def _():
        at = 0
        for ref in f_refs:
            for piece in range(ref.shape[0]):
                high, low = in_two(ref[piece])
                f_high[at : at + depth, :] = high
                f_low[at : at + depth, :] = low
                at += depth

    both = [in_two(ref[...]) for ref in k_refs]
    high = jnp.concatenate([pair[0] for pair in both], axis=1)
    low = jnp.concatenate([pair[1] for pair in both], axis=1)
    dot = functools.partial(jnp.dot, preferred_element_type=jnp.float32)
    total = dot(low, f_high[...]) + dot(high, f_low[...])
    total = total + dot(high, f_high[...])
    if accumulate:
        total = total + before[0]
    out_ref[0] = total


def multiply(table, k, pieces, chunk, chunks, before):
    rows, owners = k.shape[0], sum(array.shape[0] for array in pieces)
    depth, width = pieces[0].shape[1:]
    tile = rows // 3

    def block(piece):
        return pl.BlockSpec(
            (tile, depth), lambda m, table: (m, table[piece] * chunks + chunk)
        )

    whole = [pl.BlockSpec(a.shape, lambda m, table: (0, 0, 0)) for a in pieces]
    place = pl.BlockSpec((1, tile, width), lambda m, table: (0, m, 0))
    accumulate = before is not None
    extra = [before] if accumulate else []
    return pl.pallas_call(
        functools.partial(multiply_kernel, owners, len(pieces), accumulate),
        grid_spec=pltpu.PrefetchScalarGridSpec(
            num_scalar_prefetch=1,
            grid=(rows // tile,),
            in_specs=[block(piece) for piece in range(owners)] + whole + [place] * len(extra),
            out_specs=place,
            scratch_shapes=[pltpu.VMEM((owners * depth, width), HALF)] * 2,
        ),
        out_shape=jax.ShapeDtypeStruct((1, rows, width), jnp.float32),
        input_output_aliases={1 + owners + len(pieces): 0} if accumulate else {},
        cost_estimate=pl.CostEstimate(
            flops=6 * rows * owners * depth * width,
            bytes_accessed=4 * rows * (owners * depth + width),
            transcendentals=0,
        ),
        compiler_params=pltpu.CompilerParams(vmem_limit_bytes=40 * 2**20),
        name="multiply_sources",
    )(table, *[k] * owners, *pieces, *extra)


def body(densities, reduced_kernel):
    levels = lax.axis_size("irrep").bit_length() - 1
    bits = lax.axis_size("row").bit_length() - 2
    mine, k = densities[0], reduced_kernel[0]
    chunks = 2
    depth = mine.shape[0] // chunks
    table = owner_table(bits)
    out = None
    for chunk in range(chunks):
        folded = fold(mine[chunk * depth : (chunk + 1) * depth], levels)
        own = gather_chips(folded, bits)
        other = exchange(own, [1, 1])
        out = multiply(table, k, [own, other], chunk, chunks, out)
    return out


def solution(mesh):
    placed = (P("irrep", "row", None), P("irrep", "row", None))
    return jax.shard_map(
        body, mesh=mesh, in_specs=placed, out_specs=P("irrep", "row", None), check_vma=False
    )
```

time: 138 us -> 76.1 us (0.55)
  the two profiles are of different devices: /device:TPU:0 before, /device:TPU:25 now
where the time goes in v2:
time: 76.1 us; the launch traced here: 75.9 us
  waiting for transfers between devices  27.5 us (36%)
  starting transfers between devices  26.7 us (35%)
  Pallas kernels  19 us (25%)
  other arithmetic  1.42 us (2%)
  local copies, waits for them, and re-layouts  1.15 us (2%)
    ppermute x10, waiting for transfers between devices, exchange(): return lax.ppermute(value, AXES, pairs)  27.5 us
    ppermute x10, starting transfers between devices, exchange(): return lax.ppermute(value, AXES, pairs)  26.7 us
    pallas_call x2, Pallas kernels, multiply(): pl.pallas_call(functools.partial(multiply_kernel, owners, len(pieces), ac...  19 us
  transfers between devices with their start and end apart: 10, of which 6 were waited for; matrix products, arithmetic and copies ran while one was open for 0% of the time, Pallas kernels for 12%

profile of v2, /device:TPU:25, one launch (start us, length us, event | category | flops | bytes accessed | tf_op | source)
XLA Modules:
  0.0 75.9 jit_solution(13584657830264091804)
XLA Ops:
  0.0 1.1 %slice_bitcast_fusion = (f32[128,512]{1,0:T(8,128)S(1)}, f32[128,512]{1,0:T(8,128)S(1)}) fusion(f32[1,256,512]{2,1,0:T(8,128)} %param.2), kind=kLoop, calls=%fused_computation.6 | loop fusion | bytes 1048576 | tf_op jit(solution)/shard_map/slice | solution.py:137
  1.1 0.1 collective-permute-start.5
  1.2 2.3 %collective-permute-start = (f32[128,512]{1,0:T(8,128)S(1)}, f32[128,512]{1,0:T(8,128)S(1)}, u32[]{:S(2)}, u32[]{:S(2)}) collective-permute-start(f32[128,512]{1,0:T(8,128)S(1)} %get-tuple-element.8), channel_id=1, source_target_pairs={{0,8},{1,17},{2,10},{3,19},{4,12},{5,21},{6,14},{7,23},{8,0},{9,25... | collective-permute-start | bytes 786440 | tf_op jit(solution)/shard_map/ppermute | solution.py:18
  3.5 6.6 %collective-permute-done.5 = f32[128,512]{1,0:T(8,128)S(1)} collective-permute-done((f32[128,512]{1,0:T(8,128)S(1)}, f32[128,512]{1,0:T(8,128)S(1)}, u32[]{:S(2)}, u32[]{:S(2)}) %collective-permute-start.5) | collective-permute-done | bytes 262176 | tf_op jit(solution)/shard_map/ppermute | solution.py:18
  10.1 5.6 %collective-permute-done = f32[128,512]{1,0:T(8,128)S(1)} collective-permute-done((f32[128,512]{1,0:T(8,128)S(1)}, f32[128,512]{1,0:T(8,128)S(1)}, u32[]{:S(2)}, u32[]{:S(2)}) %collective-permute-start) | collective-permute-done | bytes 262176 | tf_op jit(solution)/shard_map/ppermute | solution.py:18
  15.7 1.1 %add_select_fusion = (f32[128,512]{1,0:T(8,128)S(1)}, f32[128,512]{1,0:T(8,128)S(1)}) fusion(f32[128,512]{1,0:T(8,128)S(1)} %collective-permute-done.5, pred[]{:T(512)S(6)} %eq.11, f32[1,256,512]{2,1,0:T(8,128)} %param.2, f32[128,512]{1,0:T(8,128)S(1)} %collective-permute-done), kind=kLoop, calls=%fused_computation.5 | loop fusion | flops 393216 | bytes 1572865 | tf_op jit(solution)/shard_map/jit(_where)/select_n | solution.py:32
  16.8 0.1 collective-permute-start.6
  16.9 5.9 %collective-permute-done.6 = f32[128,512]{1,0:T(8,128)S(1)} collective-permute-done((f32[128,512]{1,0:T(8,128)S(1)}, f32[128,512]{1,0:T(8,128)S(1)}, u32[]{:S(2)}, u32[]{:S(2)}) %collective-permute-start.6) | collective-permute-done | bytes 262176 | tf_op jit(solution)/shard_map/ppermute | solution.py:18
  22.8 1.3 %collective-permute-start.7 = (f32[1,128,512]{2,1,0:T(8,128)S(1)}, f32[1,128,512]{2,1,0:T(8,128)S(1)}, u32[]{:S(2)}, u32[]{:S(2)}) collective-permute-start(f32[1,128,512]{2,1,0:T(8,128)S(1)} %multiply_bitcast_fusion), channel_id=1, source_target_pairs={{0,2},{1,5},{2,0},{3,7},{4,6},{5,1},{6,4},{7,3},{8,10},{9,13},{10,... | collective-permute-start | bytes 786440 | tf_op jit(solution)/shard_map/ppermute | solution.py:18
  24.1 1.1 %collective-permute-start.1 = (f32[128,512]{1,0:T(8,128)S(1)}, f32[128,512]{1,0:T(8,128)S(1)}, u32[]{:S(2)}, u32[]{:S(2)}) collective-permute-start(f32[128,512]{1,0:T(8,128)S(1)} %get-tuple-element.6), channel_id=1, source_target_pairs={{0,16},{1,9},{2,18},{3,11},{4,20},{5,13},{6,22},{7,15},{8,24},{9,1... | collective-permute-start | bytes 786440 | tf_op jit(solution)/shard_map/ppermute | solution.py:18
  25.3 2.8 %collective-permute-done.7 = f32[1,128,512]{2,1,0:T(8,128)S(1)} collective-permute-done((f32[1,128,512]{2,1,0:T(8,128)S(1)}, f32[1,128,512]{2,1,0:T(8,128)S(1)}, u32[]{:S(2)}, u32[]{:S(2)}) %collective-permute-start.7) | collective-permute-done | bytes 262176 | tf_op jit(solution)/shard_map/ppermute | solution.py:18
  28.2 1.3 %collective-permute-start.8 = (f32[2,128,512]{2,1,0:T(8,128)S(1)}, f32[2,128,512]{2,1,0:T(8,128)S(1)}, u32[]{:S(2)}, u32[]{:S(2)}) collective-permute-start(f32[2,128,512]{2,1,0:T(8,128)S(1)} %pad_maximum_fusion.3), channel_id=1, source_target_pairs={{0,4},{1,3},{2,6},{3,1},{4,0},{5,7},{6,2},{7,5},{8,12},{9,11},{10,... | collective-permute-start | bytes 1572872 | tf_op jit(solution)/shard_map/ppermute | solution.py:18
  29.4 0.0 collective-permute-done.1
  29.5 1.3 %collective-permute-start.2 = (f32[1,128,512]{2,1,0:T(8,128)S(1)}, f32[1,128,512]{2,1,0:T(8,128)S(1)}, u32[]{:S(2)}, u32[]{:S(2)}) collective-permute-start(f32[1,128,512]{2,1,0:T(8,128)S(1)} %multiply_bitcast_fusion.1), channel_id=1, source_target_pairs={{0,2},{1,5},{2,0},{3,7},{4,6},{5,1},{6,4},{7,3},{8,10},{9,13},{10,... | collective-permute-start | bytes 786440 | tf_op jit(solution)/shard_map/ppermute | solution.py:18
  30.8 4.3 %collective-permute-done.2 = f32[1,128,512]{2,1,0:T(8,128)S(1)} collective-permute-done((f32[1,128,512]{2,1,0:T(8,128)S(1)}, f32[1,128,512]{2,1,0:T(8,128)S(1)}, u32[]{:S(2)}, u32[]{:S(2)}) %collective-permute-start.2) | collective-permute-done | bytes 262176 | tf_op jit(solution)/shard_map/ppermute | solution.py:18
  35.1 1.2 %collective-permute-start.3 = (f32[2,128,512]{2,1,0:T(8,128)S(1)}, f32[2,128,512]{2,1,0:T(8,128)S(1)}, u32[]{:S(2)}, u32[]{:S(2)}) collective-permute-start(f32[2,128,512]{2,1,0:T(8,128)S(1)} %pad_maximum_fusion.2), channel_id=1, source_target_pairs={{0,4},{1,3},{2,6},{3,1},{4,0},{5,7},{6,2},{7,5},{8,12},{9,11},{10,... | collective-permute-start | bytes 1572872 | tf_op jit(solution)/shard_map/ppermute | solution.py:18
  36.3 2.3 %collective-permute-done.8 = f32[2,128,512]{2,1,0:T(8,128)S(1)} collective-permute-done((f32[2,128,512]{2,1,0:T(8,128)S(1)}, f32[2,128,512]{2,1,0:T(8,128)S(1)}, u32[]{:S(2)}, u32[]{:S(2)}) %collective-permute-start.8) | collective-permute-done | bytes 524320 | tf_op jit(solution)/shard_map/ppermute | solution.py:18
  38.7 0.1 pad_maximum_fusion.1.refs_8_
  38.7 9.2 %collective-permute-start.9 = (f32[4,128,512]{2,1,0:T(8,128)S(1)}, f32[4,128,512]{2,1,0:T(8,128)S(1)}, u32[]{:S(2)}, u32[]{:S(2)}) collective-permute-start(f32[4,128,512]{2,1,0:T(8,128)S(1)} %pad_maximum_fusion.1.refs_8_), channel_id=1, source_target_pairs={{0,1},{1,0},{2,3},{3,2},{4,5},{5,4},{6,7},{7,6},{8,9},{9,8},{10,11... | collective-permute-start | bytes 3145736 | tf_op jit(solution)/shard_map/ppermute | solution.py:18
  48.0 0.0 collective-permute-done.3
  48.0 0.1 pad_maximum_fusion.refs_8_
  48.1 8.7 %collective-permute-start.4 = (f32[4,128,512]{2,1,0:T(8,128)S(1)}, f32[4,128,512]{2,1,0:T(8,128)}, u32[]{:S(2)}, u32[]{:S(2)}) collective-permute-start(f32[4,128,512]{2,1,0:T(8,128)S(1)} %pad_maximum_fusion.refs_8_), channel_id=1, source_target_pairs={{0,1},{1,0},{2,3},{3,2},{4,5},{5,4},{6,7},{7,6},{8,9},{9,8},{10,11... | collective-permute-start | bytes 3145736 | tf_op jit(solution)/shard_map/ppermute | solution.py:18
  56.8 0.1 stack.35.table_ref
  56.9 0.0 collective-permute-done.9.refs_9_
  56.9 9.0 %multiply_sources.2.refs_10_ = f32[1,1536,512]{2,1,0:T(8,128)} custom-call(s32[8]{0:T(128)S(1)} %stack.35.table_ref, f32[1536,2048]{1,0:T(8,128)} %bitcast.21, f32[1536,2048]{1,0:T(8,128)} %bitcast.22, f32[1536,2048]{1,0:T(8,128)} %bitcast.23, f32[1536,2048]{1,0:T(8,128)} %bitcast.24, f32[1536,2048]{1,0:T(8,128)} %bitcast.25, f32[1536,2048]{1,0:T(8,128)} %bitcast.26, ...), custom_call_target="tpu_custom_call" | custom-call | flops 4831838208 | bytes 9437184 | tf_op jit(solution)/shard_map/multiply_sources/pallas_call | solution.py:107
  65.9 0.0 collective-permute-done.4.refs_9_
  65.9 10.0 %multiply_sources.3 = f32[1,1536,512]{2,1,0:T(8,128)} custom-call(s32[8]{0:T(128)S(1)} %stack.35.table_ref, f32[1536,2048]{1,0:T(8,128)} %bitcast.29, f32[1536,2048]{1,0:T(8,128)} %bitcast.30, f32[1536,2048]{1,0:T(8,128)} %bitcast.31, f32[1536,2048]{1,0:T(8,128)} %bitcast.32, f32[1536,2048]{1,0:T(8,128)} %bitcast.33, ...), custom_call_target="tpu_custom_call", output_to_operand_aliasing={{}: (11, {})} | custom-call | flops 4831838208 | bytes 9437184 | tf_op jit(solution)/shard_map/multiply_sources/pallas_call | solution.py:107
  (4 shorter events, 0.2 us)
Async XLA Ops:
  1.1 9.0 %collective-permute-start.5 = (f32[128,512]{1,0:T(8,128)S(1)}, f32[128,512]{1,0:T(8,128)S(1)}, u32[]{:S(2)}, u32[]{:S(2)}) collective-permute-start(f32[128,512]{1,0:T(8,128)S(1)} %get-tuple-element.7), channel_id=1, source_target_pairs={{0,8},{1,17},{2,10},{3,19},{4,12},{5,21},{6,14},{7,23},{8,0},{9,25... | collective-permute-start | bytes 786440 | tf_op jit(solution)/shard_map/ppermute | solution.py:18
  1.2 14.5 %collective-permute-start = (f32[128,512]{1,0:T(8,128)S(1)}, f32[128,512]{1,0:T(8,128)S(1)}, u32[]{:S(2)}, u32[]{:S(2)}) collective-permute-start(f32[128,512]{1,0:T(8,128)S(1)} %get-tuple-element.8), channel_id=1, source_target_pairs={{0,8},{1,17},{2,10},{3,19},{4,12},{5,21},{6,14},{7,23},{8,0},{9,25... | collective-permute-start | bytes 786440 | tf_op jit(solution)/shard_map/ppermute | solution.py:18
  16.8 6.0 %collective-permute-start.6 = (f32[128,512]{1,0:T(8,128)S(1)}, f32[128,512]{1,0:T(8,128)S(1)}, u32[]{:S(2)}, u32[]{:S(2)}) collective-permute-start(f32[128,512]{1,0:T(8,128)S(1)} %get-tuple-element.5), channel_id=1, source_target_pairs={{0,16},{1,9},{2,18},{3,11},{4,20},{5,13},{6,22},{7,15},{8,24},{9,1... | collective-permute-start | bytes 786440 | tf_op jit(solution)/shard_map/ppermute | solution.py:18
  22.8 5.3 %collective-permute-start.7 = (f32[1,128,512]{2,1,0:T(8,128)S(1)}, f32[1,128,512]{2,1,0:T(8,128)S(1)}, u32[]{:S(2)}, u32[]{:S(2)}) collective-permute-start(f32[1,128,512]{2,1,0:T(8,128)S(1)} %multiply_bitcast_fusion), channel_id=1, source_target_pairs={{0,2},{1,5},{2,0},{3,7},{4,6},{5,1},{6,4},{7,3},{8,10},{9,13},{10,... | collective-permute-start | bytes 786440 | tf_op jit(solution)/shard_map/ppermute | solution.py:18
  24.1 5.3 %collective-permute-start.1 = (f32[128,512]{1,0:T(8,128)S(1)}, f32[128,512]{1,0:T(8,128)S(1)}, u32[]{:S(2)}, u32[]{:S(2)}) collective-permute-start(f32[128,512]{1,0:T(8,128)S(1)} %get-tuple-element.6), channel_id=1, source_target_pairs={{0,16},{1,9},{2,18},{3,11},{4,20},{5,13},{6,22},{7,15},{8,24},{9,1... | collective-permute-start | bytes 786440 | tf_op jit(solution)/shard_map/ppermute | solution.py:18
  28.2 10.5 %collective-permute-start.8 = (f32[2,128,512]{2,1,0:T(8,128)S(1)}, f32[2,128,512]{2,1,0:T(8,128)S(1)}, u32[]{:S(2)}, u32[]{:S(2)}) collective-permute-start(f32[2,128,512]{2,1,0:T(8,128)S(1)} %pad_maximum_fusion.3), channel_id=1, source_target_pairs={{0,4},{1,3},{2,6},{3,1},{4,0},{5,7},{6,2},{7,5},{8,12},{9,11},{10,... | collective-permute-start | bytes 1572872 | tf_op jit(solution)/shard_map/ppermute | solution.py:18
  29.5 5.6 %collective-permute-start.2 = (f32[1,128,512]{2,1,0:T(8,128)S(1)}, f32[1,128,512]{2,1,0:T(8,128)S(1)}, u32[]{:S(2)}, u32[]{:S(2)}) collective-permute-start(f32[1,128,512]{2,1,0:T(8,128)S(1)} %multiply_bitcast_fusion.1), channel_id=1, source_target_pairs={{0,2},{1,5},{2,0},{3,7},{4,6},{5,1},{6,4},{7,3},{8,10},{9,13},{10,... | collective-permute-start | bytes 786440 | tf_op jit(solution)/shard_map/ppermute | solution.py:18
  35.1 12.9 %collective-permute-start.3 = (f32[2,128,512]{2,1,0:T(8,128)S(1)}, f32[2,128,512]{2,1,0:T(8,128)S(1)}, u32[]{:S(2)}, u32[]{:S(2)}) collective-permute-start(f32[2,128,512]{2,1,0:T(8,128)S(1)} %pad_maximum_fusion.2), channel_id=1, source_target_pairs={{0,4},{1,3},{2,6},{3,1},{4,0},{5,7},{6,2},{7,5},{8,12},{9,11},{10,... | collective-permute-start | bytes 1572872 | tf_op jit(solution)/shard_map/ppermute | solution.py:18
  38.7 18.1 %collective-permute-start.9 = (f32[4,128,512]{2,1,0:T(8,128)S(1)}, f32[4,128,512]{2,1,0:T(8,128)S(1)}, u32[]{:S(2)}, u32[]{:S(2)}) collective-permute-start(f32[4,128,512]{2,1,0:T(8,128)S(1)} %pad_maximum_fusion.1.refs_8_), channel_id=1, source_target_pairs={{0,1},{1,0},{2,3},{3,2},{4,5},{5,4},{6,7},{7,6},{8,9},{9,8},{10,11... | collective-permute-start | bytes 3145736 | tf_op jit(solution)/shard_map/ppermute | solution.py:18
  48.1 17.8 %collective-permute-start.4 = (f32[4,128,512]{2,1,0:T(8,128)S(1)}, f32[4,128,512]{2,1,0:T(8,128)}, u32[]{:S(2)}, u32[]{:S(2)}) collective-permute-start(f32[4,128,512]{2,1,0:T(8,128)S(1)} %pad_maximum_fusion.refs_8_), channel_id=1, source_target_pairs={{0,1},{1,0},{2,3},{3,2},{4,5},{5,4},{6,7},{7,6},{8,9},{9,8},{10,11... | collective-permute-start | bytes 3145736 | tf_op jit(solution)/shard_map/ppermute | solution.py:18
